TPU v7x, 128 devices: a whole 4x4x4 slice. The times are simulated.
128 devices in a mesh: scene: 8 (over y, core), frame: 16 (over z, x).
Axes of the slice: x: 4, y: 4, z: 4, core: 2. Of those that a mesh axis runs over, the one named last changes fastest.
Arguments:
- occupancy: bfloat16 [8, 64, 64, 2048], P('scene', 'frame'), may hold values from -6 to 6
- scene_lengths: int32 [8], P('scene'), may hold values from 8 to 64, as said below
- conv1_weight: bfloat16 [128, 1728], replicated, may hold values from -0.15625 to 0.15625
- conv2_weight: bfloat16 [256, 3456], replicated, may hold values from -0.109375 to 0.109375
- temporal_weight: bfloat16 [3, 256, 256], replicated, may hold values from -0.21875 to 0.21875
- query_weight: bfloat16 [256, 256], replicated
- key_weight: bfloat16 [256, 256], replicated
- value_weight: bfloat16 [256, 256], replicated, may hold values from -0.375 to 0.375
- out_weight: bfloat16 [256, 256], replicated, may hold values from -0.375 to 0.375
Outputs:
- encoded: bfloat16 [8, 64, 256, 512], P('scene', 'frame')
- kl_loss: float32 [], replicated
Inputs may be any that keep to these rules, and one draw needn't show every extreme that they name: `scene_lengths`: non-decreasing along the scenes; the first scene has exactly 8 frames with data and the last exactly 64.
All inputs are finite; a program needn't handle non-finite values.
Results may differ from a plain program's by a relative error of at most 0.011.
Values may be sent and summed in bfloat16 or wider, within the bound.
A program may use at most 192 MiB of HBM per device.

v0:
```python
import jax
import jax.numpy as jnp
from jax import lax
from jax.sharding import PartitionSpec as P

CIN = 64
C1 = 128
C2 = 256
HEADS = 4
HD = 64
HI = 16
ZD = 8
CELLS = 512
NORM_EPS = 1e-06


def extended(cells, sides, width):
    for axis, dim in sides:
        count = lax.axis_size(axis)
        ends = count - 1
        head = lax.slice_in_dim(cells, 0, width, axis=dim)
        tail = lax.slice_in_dim(cells, cells.shape[dim] - width, cells.shape[dim], axis=dim)
        cells = jnp.concatenate(
            [
                lax.ppermute(tail, axis, [(i, (i + 1) % count) for i in range(ends)]),
                cells,
                lax.ppermute(head, axis, [((i + 1) % count, i) for i in range(ends)]),
            ],
            axis=dim,
        )
    return cells


def spatial_conv(voxels, weight, channels_in, stride):
    channels_out = weight.shape[0]
    kernel = weight.reshape(channels_out, channels_in, 3, 3, 3)
    return lax.conv_general_dilated(
        voxels,
        kernel,
        (stride, stride, 1),
        ((1, 1), (1, 1), (1, 1)),
        dimension_numbers=("NCDHW", "OIDHW", "NCDHW"),
        preferred_element_type=jnp.float32,
    )


def mix_channels(weight, maps):
    return jnp.einsum("oc,fcn->fon", weight, maps, preferred_element_type=jnp.float32)


def temporal_block(padded, second_maps, temporal_weight):
    count_frames = second_maps.shape[0]
    temporal_sum = mix_channels(temporal_weight[0], padded[0:count_frames])
    for tap in range(1, 3):
        temporal_sum = temporal_sum + mix_channels(
            temporal_weight[tap], padded[tap : tap + count_frames]
        )
    residual_maps = (second_maps.astype(jnp.float32) + jax.nn.silu(temporal_sum)).astype(
        jnp.bfloat16
    )
    return residual_maps.astype(jnp.float32)


def project_rows(residual_f, query_weight, key_weight, value_weight):
    count_frames = residual_f.shape[0]
    count_cells = residual_f.shape[2]
    normed = (
        residual_f * lax.rsqrt(jnp.mean(residual_f * residual_f, axis=1, keepdims=True) + NORM_EPS)
    ).astype(jnp.bfloat16)
    queries = (
        mix_channels(query_weight, normed)
        .astype(jnp.bfloat16)
        .reshape(count_frames, HEADS, HD, count_cells)
    )
    key_rows = (
        mix_channels(key_weight, normed)
        .astype(jnp.bfloat16)
        .reshape(count_frames, HEADS, HD, count_cells)
    )
    value_rows = (
        mix_channels(value_weight, normed)
        .astype(jnp.bfloat16)
        .reshape(count_frames, HEADS, HD, count_cells)
    )
    return (queries, key_rows, value_rows)


def finish_rows(residual_f, attended, out_weight, valid_rows):
    count_frames = residual_f.shape[0]
    count_cells = residual_f.shape[2]
    out_full = residual_f + mix_channels(
        out_weight, attended.reshape(count_frames, C2, count_cells)
    )
    return (out_full * valid_rows[:, None, None]).astype(jnp.bfloat16)


def shards(
    occupancy,
    scene_lengths,
    conv1_weight,
    conv2_weight,
    temporal_weight,
    query_weight,
    key_weight,
    value_weight,
    out_weight,
):
    f_dev = occupancy.shape[1]
    length = scene_lengths[0]
    first_frame = lax.axis_index("frame") * f_dev
    frame_ids = first_frame + jnp.arange(f_dev, dtype=jnp.int32)
    valid_rows = (frame_ids < length).astype(jnp.float32)
    voxels = occupancy[0].reshape(f_dev, CIN, HI, HI, ZD)
    first_maps = jax.nn.silu(spatial_conv(voxels, conv1_weight, CIN, 2)).astype(jnp.bfloat16)
    second_full = jax.nn.silu(spatial_conv(first_maps, conv2_weight, C1, 1))
    second_maps = (second_full.reshape(f_dev, C2, CELLS) * valid_rows[:, None, None]).astype(
        jnp.bfloat16
    )
    padded = extended(second_maps, (("frame", 0),), 1)
    residual_f = temporal_block(padded, second_maps, temporal_weight)
    queries, key_rows, value_rows = project_rows(residual_f, query_weight, key_weight, value_weight)
    running_max = jnp.full((f_dev, HEADS, CELLS), -1e30, jnp.float32)
    panel_keys = lax.all_gather(key_rows, "frame", axis=0, tiled=True)
    panel_values = lax.all_gather(value_rows, "frame", axis=0, tiled=True)
    count_keys = panel_keys.shape[0]
    scores = jnp.einsum(
        "qhdc,khdc->qkhc", queries, panel_keys, preferred_element_type=jnp.float32
    ) * HD ** (-0.5)
    key_mask = (jnp.arange(count_keys) < length)[None, :, None, None]
    scores = jnp.where(key_mask, scores, -1e30)
    new_max = jnp.maximum(running_max, jnp.max(scores, axis=1))
    raw_weights = jnp.where(key_mask, jnp.exp(scores - new_max[:, None]), 0.0)
    new_sum = jnp.sum(raw_weights, axis=1)
    addition = jnp.einsum(
        "qkhc,khdc->qhdc",
        raw_weights.astype(jnp.bfloat16),
        panel_values,
        preferred_element_type=jnp.float32,
    )
    attended = (addition / new_sum[:, :, None, :]).astype(jnp.bfloat16)
    encoded = finish_rows(residual_f, attended, out_weight, valid_rows)
    squares = jnp.sum(jnp.square(encoded.astype(jnp.float32)))
    grand_total = lax.psum(squares, ("scene", "frame"))
    slot_count = float(lax.axis_size("scene") * lax.axis_size("frame") * f_dev * CELLS * C2)
    kl_loss = 0.5 * grand_total / slot_count
    return (encoded[None], kl_loss)


def solution(mesh):
    placed = (P("scene", "frame", None, None), P("scene"), P(), P(), P(), P(), P(), P(), P())
    return jax.shard_map(
        shards,
        mesh=mesh,
        in_specs=placed,
        out_specs=(P("scene", "frame", None, None), P()),
        check_vma=False,
    )
```

profile of v0, /device:TPU:1, one launch (start us, length us, event | category | flops | bytes accessed | tf_op | source)
XLA Modules:
  0.0 420.5 jit_solution(17460069256639030074)
XLA Ops:
  7.9 2.6 copy.62
  10.6 2.9 reshape.49
  14.5 1.5 reshape.48
  16.0 5.0 %fusion.28 = bf16[4,128,8,8,8]{1,0,4,3,2:T(4,128)(2,1)S(1)} fusion(bf16[4,64,16,16,8]{1,4,3,2,0:T(8,128)(2,1)S(1)} %bitcast.90, bf16[128,64,3,3,3]{0,4,3,2,1:T(4,128)(2,1)S(1)} %reshape.48), kind=kOutput, calls=%fused_computation.44 | convolution fusion | flops 764018688 | bytes 2015232 | tf_op jit(solution)/shard_map/conv_general_dilated | solution.py:37
  21.0 7.9 %multiply_convert_fusion = (bf16[4,256,8,8,8]{1,0,4,3,2:T(4,128)(2,1)S(1)}, f32[4,256,8,8,8]{1,0,4,3,2:T(4,128)}) fusion(f32[4]{0:T(128)S(1)} %compare_convert_fusion, bf16[4,128,8,8,8]{1,0,4,3,2:T(4,128)(2,1)S(1)} %fusion.28, bf16[256,128,3,3,3]{0,4,3,2,1:T(4,128)(2,1)S(1)} %copy-done.1), kind=kOutput, calls=%fused_computation.24 | convolution fusion | flops 2794455040 | bytes 5439504 | tf_op jit(solution)/shard_map/conv_general_dilated | solution.py:37
  28.9 1.9 copy.64
  31.2 4.0 collective-permute-start
  35.1 1.5 collective-permute-start.1
  37.1 3.0 collective-permute-done
  40.5 3.4 collective-permute-done.1
  45.0 1.4 convolution_convert_fusion.1
  46.5 1.4 convolution_convert_fusion.2
  48.4 2.5 copy.67
  50.9 112.4 %all-gather.5.cloned.1.call-done = bf16[64,4,64,512]{3,2,1,0:T(8,128)(2,1)} async-done(((bf16[4,4,64,512]{3,2,1,0:T(8,128)(2,1)}), bf16[64,4,64,512]{3,2,1,0:T(8,128)(2,1)}) %all-gather.5.cloned.1.call-update) | async-done | bytes 16777232 | tf_op jit(solution)/shard_map/all_gather | solution.py:123
  163.3 46.8 %copy.66 = bf16[64,4,64,512]{2,0,3,1:T(8,128)(2,1)} copy(bf16[64,4,64,512]{3,2,1,0:T(8,128)(2,1)} %all-gather.5.cloned.1.call-done) | data formatting | bytes 33554432 | tf_op jit(solution)/shard_map/all_gather | solution.py:123
  210.1 24.4 %bitcast_reduce_fusion = (f32[4,4,512]{0,2,1:T(8,128)}, f32[4,512,64,4]{2,3,1,0:T(4,128)}) fusion(pred[64]{0:T(512)(128)(4,1)S(1)} %iota_compare_fusion, bf16[64,4,64,512]{2,0,3,1:T(8,128)(2,1)} %copy.66, bf16[4,4,64,512]{2,0,3,1:T(4,128)(2,1)S(1)} %copy-done.2), kind=kOutput, calls=%fused_computation.1 | convolution fusion | flops 68673536 | bytes 19955776 | tf_op jit(solution)/shard_map/qhdc,khdc->qkhc/dot_general | solution.py:126
  234.5 1.4 broadcast_maximum_fusion
  235.9 30.0 %fusion.20 = f32[4,4,512]{0,2,1:T(8,128)S(1)} fusion(f32[4,4,512]{0,2,1:T(8,128)S(1)} %broadcast_maximum_fusion, f32[4,512,64,4]{2,3,1,0:T(4,128)} %get-tuple-element.9, pred[64]{0:T(512)(128)(4,1)S(1)} %iota_compare_fusion), kind=kLoop, calls=%fused_computation.34 | loop fusion | flops 2613248 | bytes 2162752 | tf_op jit(solution)/shard_map/reduce_sum | solution.py:133
  266.2 10.9 %all-gather.3.cloned.1.call-done = bf16[64,4,64,512]{3,2,1,0:T(8,128)(2,1)} async-done(((bf16[4,4,64,512]{3,2,1,0:T(8,128)(2,1)}), bf16[64,4,64,512]{3,2,1,0:T(8,128)(2,1)}) %all-gather.3.cloned.1.call-update) | async-done | bytes 16777232 | tf_op jit(solution)/shard_map/all_gather | solution.py:124
  277.1 46.6 %copy.68 = bf16[64,4,64,512]{2,0,3,1:T(8,128)(2,1)} copy(bf16[64,4,64,512]{3,2,1,0:T(8,128)(2,1)} %all-gather.3.cloned.1.call-done) | data formatting | bytes 33554432 | tf_op jit(solution)/shard_map/all_gather | solution.py:124
  323.7 17.5 %fusion.11 = f32[4,512,64,4]{2,3,1,0:T(4,128)} fusion(bf16[64,4,64,512]{2,0,3,1:T(8,128)(2,1)} %copy.68, f32[4,512,64,4]{2,3,1,0:T(4,128)} %get-tuple-element.9, f32[4,4,512]{0,2,1:T(8,128)S(1)} %broadcast_maximum_fusion, pred[64]{0:T(512)(128)(4,1)S(1)} %iota_compare_fusion), kind=kOutput, calls=%fused_computation.22 | convolution fusion | flops 69730304 | bytes 21004352 | tf_op jit(solution)/shard_map/qkhc,khdc->qhdc/dot_general | solution.py:134
  341.2 3.5 copy.69
  345.0 2.3 multiply_reduce_fusion
  347.3 64.6 %psum.7 = f32[]{:T(128)} all-reduce(f32[]{:T(128)} %get-tuple-element.10), channel_id=1, replica_groups=mesh['scene'=8,'frame'=16] {'scene','frame'}, use_global_device_ids=true, to_apply=%region_4.5 | all-reduce | flops 1 | bytes 8 | tf_op jit(solution)/shard_map/psum | solution.py:143
  (32 shorter events, 4.7 us)
Async XLA Ops:
  7.2 337.9 %copy-start = (bf16[256,256]{1,0:T(8,128)(2,1)S(1)}, bf16[256,256]{1,0:T(8,128)(2,1)}, u32[]{:S(2)}) copy-start(bf16[256,256]{1,0:T(8,128)(2,1)} %param.17) | copy-start | bytes 393220
  7.2 156.1 %all-gather.5.cloned.1.call-start = ((), (), s32[]{:S(2)}) async-start(), calls=%async_computation.1 | async-start | bytes 17825792 | tf_op jit(solution)/shard_map/all_gather | solution.py:123
  10.5 2.9 copy-start.3
  16.0 5.0 %copy-start.1 = (bf16[256,128,3,3,3]{0,4,3,2,1:T(4,128)(2,1)S(1)}, bf16[256,128,3,3,3]{0,4,3,2,1:T(4,128)(2,1)}, u32[]{:S(2)}) copy-start(bf16[256,128,3,3,3]{0,4,3,2,1:T(4,128)(2,1)} %reshape.49) | copy-start | bytes 5308420
  30.8 5.8 %copy-start.4 = (bf16[3,256,256]{2,1,0:T(8,128)(2,1)S(1)}, bf16[3,256,256]{2,1,0:T(8,128)(2,1)}, u32[]{:S(2)}) copy-start(bf16[3,256,256]{2,1,0:T(8,128)(2,1)} %param.13) | copy-start | bytes 1179652
  31.2 8.9 %collective-permute-start = (bf16[1,256,512]{2,1,0:T(8,128)(2,1)S(1)}, bf16[1,256,512]{2,1,0:T(8,128)(2,1)S(1)}, u32[]{:S(2)}, u32[]{:S(2)}) collective-permute-start(bf16[1,256,512]{2,1,0:T(8,128)(2,1)S(1)} %get-tuple-element.3), channel_id=1, source_target_pairs={{0,1},{1,2},{2,3},{3,4},{4,5},{5,6},{6,7},{7,8},{8,9},{9,10},{10,1... | collective-permute-start | bytes 786440 | tf_op jit(solution)/shard_map/ppermute | solution.py:25
  35.1 8.7 %collective-permute-start.1 = (bf16[1,256,512]{2,1,0:T(8,128)(2,1)S(1)}, bf16[1,256,512]{2,1,0:T(8,128)(2,1)S(1)}, u32[]{:S(2)}, u32[]{:S(2)}) collective-permute-start(bf16[1,256,512]{2,1,0:T(8,128)(2,1)S(1)} %get-tuple-element.2), channel_id=1, source_target_pairs={{1,0},{2,1},{3,2},{4,3},{5,4},{6,5},{7,6},{8,7},{9,8},{10,9},{11,1... | collective-permute-start | bytes 786440 | tf_op jit(solution)/shard_map/ppermute | solution.py:27
  40.5 4.5 %copy-start.5 = (bf16[256,256]{1,0:T(8,128)(2,1)S(1)}, bf16[256,256]{1,0:T(8,128)(2,1)}, u32[]{:S(2)}) copy-start(bf16[256,256]{1,0:T(8,128)(2,1)} %param.15) | copy-start | bytes 393220
  44.9 1.5 copy-start.6
  46.4 1.6 copy-start.7
  46.4 230.7 %all-gather.3.cloned.1.call-start = ((), (), s32[]{:S(2)}) async-start(), calls=%async_computation | async-start | bytes 17825792 | tf_op jit(solution)/shard_map/all_gather | solution.py:124
  50.9 159.2 %copy-start.2 = (bf16[4,4,64,512]{2,0,3,1:T(4,128)(2,1)S(1)}, bf16[4,4,64,512]{2,0,3,1:T(4,128)(2,1)}, u32[]{:S(2)}) copy-start(bf16[4,4,64,512]{2,0,3,1:T(4,128)(2,1)} %copy.67) | copy-start | bytes 3145732
Sparse Core Ops, SparseCore 0:
  46.6 116.7 all-gather.4
  166.0 111.0 all-gather.2
where the time goes:
time: 423 us; the launch traced here: 421 us
  waiting for transfers between devices  130 us (31%)
  local copies, waits for them, and re-layouts  110 us (26%)
  blocking collectives  64.6 us (15%)
  matrix products  62.2 us (15%)
  other arithmetic  32 us (8%)
  between operations  16.7 us (4%)
  starting transfers between devices  5.51 us (1%)
    all_gather x1, waiting for transfers between devices, shards(): panel_keys = lax.all_gather(key_rows, 'frame', axis=0, tiled=True)  112 us
    psum x1, blocking collectives, shards(): grand_total = lax.psum(squares, ('scene', 'frame'))  64.6 us
    all_gather x1, local copies, waits for them, and re-layouts, shards(): panel_keys = lax.all_gather(key_rows, 'frame', axis=0, tiled=True)  46.8 us
    all_gather x1, local copies, waits for them, and re-layouts, shards(): panel_values = lax.all_gather(value_rows, 'frame', axis=0, tiled=True)  46.6 us
    reduce_sum x1, other arithmetic, shards(): new_sum = jnp.sum(raw_weights, axis=1)  30 us
    dot_general x1, matrix products, shards(): jnp.einsum('qhdc,khdc->qkhc', queries, panel_keys, preferred_element_type...  24.4 us
    dot_general x1, matrix products, shards(): jnp.einsum('qkhc,khdc->qhdc', raw_weights.astype(jnp.bfloat16), panel_val...  17.5 us
    conv_general_dilated x2, matrix products, spatial_conv(): lax.conv_general_dilated(voxels, kernel, (stride, stride, 1), ((1, 1), (1...  12.8 us
  transfers between devices with their start and end apart: 4, of which 4 were waited for; matrix products, arithmetic and copies ran while one was open for 26% of the time, Pallas kernels for 0%

commit v1 on v0

--- a/solution.py
+++ b/solution.py
@@ -120,7 +120,9 @@
     residual_f = temporal_block(padded, second_maps, temporal_weight)
     queries, key_rows, value_rows = project_rows(residual_f, query_weight, key_weight, value_weight)
     running_max = jnp.full((f_dev, HEADS, CELLS), -1e30, jnp.float32)
-    panel_keys = lax.all_gather(key_rows, "frame", axis=0, tiled=True)
+    panel_keys = jnp.concatenate(
+        lax.all_to_all(jnp.stack([key_rows] * lax.axis_size("frame")), "frame", 0, 0), axis=0
+    )
     panel_values = lax.all_gather(value_rows, "frame", axis=0, tiled=True)
     count_keys = panel_keys.shape[0]
     scores = jnp.einsum(

time: 423 us -> 628 us (1.48)
  waiting for transfers between devices: 130 us -> 313 us
  local copies, waits for them, and re-layouts: 110 us -> 121 us
  starting transfers between devices: 5.51 us -> 15 us
    all_to_all x0 -> x1, waiting for transfers between devices: none -> 307 us  [shards(): lax.all_to_all(jnp.stack([key_rows] * lax.axis_size('frame')), 'frame', 0...]
    all_gather x1 -> x0, waiting for transfers between devices: 112 us -> none  [shards(): panel_keys = lax.all_gather(key_rows, 'frame', axis=0, tiled=True)]
    all_to_all x0 -> x1, local copies, waits for them, and re-layouts: none -> 52 us  [shards(): lax.all_to_all(jnp.stack([key_rows] * lax.axis_size('frame')), 'frame', 0...]
    all_gather x1 -> x0, local copies, waits for them, and re-layouts: 46.8 us -> none  [shards(): panel_keys = lax.all_gather(key_rows, 'frame', axis=0, tiled=True)]
    all_gather x1, waiting for transfers between devices: 10.9 us -> 0.01 us  [shards(): panel_values = lax.all_gather(value_rows, 'frame', axis=0, tiled=True)]
    all_to_all x0 -> x1, starting transfers between devices: none -> 9.49 us  [shards(): lax.all_to_all(jnp.stack([key_rows] * lax.axis_size('frame')), 'frame', 0...]
  transfers between devices with their start and end apart: 4 -> 4, of which waited for: 4 -> 3; matrix products, arithmetic and copies ran while one was open for 26% -> 19% of each run, Pallas kernels for 0% -> 0%
where the time goes in v1:
time: 628 us; the launch traced here: 625 us
  waiting for transfers between devices  313 us (50%)
  local copies, waits for them, and re-layouts  121 us (19%)
  blocking collectives  66.6 us (11%)
  matrix products  61.2 us (10%)
  other arithmetic  32 us (5%)
  between operations  16.7 us (3%)
  starting transfers between devices  15 us (2%)
    all_to_all x1, waiting for transfers between devices, shards(): lax.all_to_all(jnp.stack([key_rows] * lax.axis_size('frame')), 'frame', 0...  307 us
    psum x1, blocking collectives, shards(): grand_total = lax.psum(squares, ('scene', 'frame'))  66.6 us
    all_to_all x1, local copies, waits for them, and re-layouts, shards(): lax.all_to_all(jnp.stack([key_rows] * lax.axis_size('frame')), 'frame', 0...  52 us
    all_gather x1, local copies, waits for them, and re-layouts, shards(): panel_values = lax.all_gather(value_rows, 'frame', axis=0, tiled=True)  46.7 us
    reduce_sum x1, other arithmetic, shards(): new_sum = jnp.sum(raw_weights, axis=1)  30 us
    dot_general x1, matrix products, shards(): jnp.einsum('qhdc,khdc->qkhc', queries, panel_keys, preferred_element_type...  24.3 us
    dot_general x1, matrix products, shards(): jnp.einsum('qkhc,khdc->qhdc', raw_weights.astype(jnp.bfloat16), panel_val...  17.5 us
    conv_general_dilated x2, matrix products, spatial_conv(): lax.conv_general_dilated(voxels, kernel, (stride, stride, 1), ((1, 1), (1...  12.8 us
  transfers between devices with their start and end apart: 4, of which 3 were waited for; matrix products, arithmetic and copies ran while one was open for 19% of the time, Pallas kernels for 0%

profile of v1, /device:TPU:1, one launch (start us, length us, event | category | flops | bytes accessed | tf_op | source)
XLA Modules:
  0.0 625.3 jit_solution(18419421912157549353)
XLA Ops:
  7.9 2.6 copy.62
  10.6 2.9 reshape.51
  14.5 1.5 reshape.50
  16.0 5.0 fusion.28
  21.0 7.8 %multiply_convert_fusion = (bf16[4,256,8,8,8]{1,0,4,3,2:T(4,128)(2,1)S(1)}, f32[4,256,8,8,8]{1,0,4,3,2:T(4,128)}) fusion(f32[4]{0:T(128)S(1)} %compare_convert_fusion, bf16[4,128,8,8,8]{1,0,4,3,2:T(4,128)(2,1)S(1)} %fusion.28, bf16[256,128,3,3,3]{0,4,3,2,1:T(4,128)(2,1)S(1)} %copy-done.1), kind=kOutput, calls=%fused_computation.24 | convolution fusion | flops 2794455040 | bytes 5439504 | tf_op jit(solution)/shard_map/conv_general_dilated | solution.py:37
  28.8 1.9 copy.64
  31.2 4.0 collective-permute-start
  35.1 1.5 collective-permute-start.1
  37.1 3.0 collective-permute-done
  40.5 3.4 collective-permute-done.1
  45.0 1.4 convolution_convert_fusion.2
  46.9 5.9 stack.3
  52.8 9.5 %all-to-all-start = ((bf16[16,4,4,64,512]{4,3,2,1,0:T(8,128)(2,1)}), bf16[16,4,4,64,512]{4,3,2,1,0:T(8,128)(2,1)}, u32[]{:S(2)}, u32[]{:S(2)}) async-start(bf16[16,4,4,64,512]{4,3,2,1,0:T(8,128)(2,1)} %stack.3), calls=%async_computation | async-start | bytes 33554432 | tf_op jit(solution)/shard_map/all_to_all | solution.py:124
  62.8 2.5 copy.67
  65.3 306.6 %all-to-all-done = bf16[16,4,4,64,512]{4,3,2,1,0:T(8,128)(2,1)} async-done(((bf16[16,4,4,64,512]{4,3,2,1,0:T(8,128)(2,1)}), bf16[16,4,4,64,512]{4,3,2,1,0:T(8,128)(2,1)}, u32[]{:S(2)}, u32[]{:S(2)}) %all-to-all-start) | async-done | bytes 16777248 | tf_op jit(solution)/shard_map/all_to_all | solution.py:124
  371.9 52.0 %copy.66 = bf16[16,4,4,64,512]{3,1,0,4,2:T(4,128)(2,1)} copy(bf16[16,4,4,64,512]{4,3,2,1,0:T(8,128)(2,1)} %all-to-all-done) | data formatting | bytes 33554432 | tf_op jit(solution)/shard_map/all_to_all | solution.py:124
  423.9 24.3 %bitcast_reduce_fusion = (f32[4,4,512]{0,2,1:T(8,128)}, f32[4,512,64,4]{2,3,1,0:T(4,128)}) fusion(pred[64]{0:T(512)(128)(4,1)S(1)} %iota_compare_fusion, bf16[64,4,64,512]{2,0,3,1:T(8,128)(2,1)} %bitcast.88, bf16[4,4,64,512]{2,0,3,1:T(4,128)(2,1)S(1)} %copy-done.2), kind=kOutput, calls=%fused_computation.1 | convolution fusion | flops 68673536 | bytes 19955776 | tf_op jit(solution)/shard_map/qhdc,khdc->qkhc/dot_general | solution.py:128
  448.2 1.3 broadcast_maximum_fusion
  449.5 30.0 %fusion.20 = f32[4,4,512]{0,2,1:T(8,128)S(1)} fusion(f32[4,4,512]{0,2,1:T(8,128)S(1)} %broadcast_maximum_fusion, f32[4,512,64,4]{2,3,1,0:T(4,128)} %get-tuple-element.9, pred[64]{0:T(512)(128)(4,1)S(1)} %iota_compare_fusion), kind=kLoop, calls=%fused_computation.34 | loop fusion | flops 2613248 | bytes 2162752 | tf_op jit(solution)/shard_map/reduce_sum | solution.py:135
  479.9 46.7 %copy.68 = bf16[64,4,64,512]{2,0,3,1:T(8,128)(2,1)} copy(bf16[64,4,64,512]{3,2,1,0:T(8,128)(2,1)} %all-gather.2.cloned.1.call-done) | data formatting | bytes 33554432 | tf_op jit(solution)/shard_map/all_gather | solution.py:126
  526.6 17.5 %fusion.11 = f32[4,512,64,4]{2,3,1,0:T(4,128)} fusion(bf16[64,4,64,512]{2,0,3,1:T(8,128)(2,1)} %copy.68, f32[4,512,64,4]{2,3,1,0:T(4,128)} %get-tuple-element.9, f32[4,4,512]{0,2,1:T(8,128)S(1)} %broadcast_maximum_fusion, pred[64]{0:T(512)(128)(4,1)S(1)} %iota_compare_fusion), kind=kOutput, calls=%fused_computation.22 | convolution fusion | flops 69730304 | bytes 21004352 | tf_op jit(solution)/shard_map/qkhc,khdc->qhdc/dot_general | solution.py:136
  544.0 3.5 copy.69
  547.8 2.3 multiply_reduce_fusion
  550.1 66.6 %psum.7 = f32[]{:T(128)} all-reduce(f32[]{:T(128)} %get-tuple-element.10), channel_id=1, replica_groups=mesh['scene'=8,'frame'=16] {'scene','frame'}, use_global_device_ids=true, to_apply=%region_4.5 | all-reduce | flops 1 | bytes 8 | tf_op jit(solution)/shard_map/psum | solution.py:145
  (32 shorter events, 5.1 us)
Async XLA Ops:
  7.2 540.7 %copy-start = (bf16[256,256]{1,0:T(8,128)(2,1)S(1)}, bf16[256,256]{1,0:T(8,128)(2,1)}, u32[]{:S(2)}) copy-start(bf16[256,256]{1,0:T(8,128)(2,1)} %param.17) | copy-start | bytes 393220
  7.2 472.7 %all-gather.2.cloned.1.call-start = ((), (), s32[]{:S(2)}) async-start(), calls=%async_computation.1 | async-start | bytes 17825792 | tf_op jit(solution)/shard_map/all_gather | solution.py:126
  10.5 2.9 copy-start.3
  16.0 5.0 copy-start.1
  30.8 5.8 copy-start.4
  31.2 8.9 %collective-permute-start = (bf16[1,256,512]{2,1,0:T(8,128)(2,1)S(1)}, bf16[1,256,512]{2,1,0:T(8,128)(2,1)S(1)}, u32[]{:S(2)}, u32[]{:S(2)}) collective-permute-start(bf16[1,256,512]{2,1,0:T(8,128)(2,1)S(1)} %get-tuple-element.3), channel_id=1, source_target_pairs={{0,1},{1,2},{2,3},{3,4},{4,5},{5,6},{6,7},{7,8},{8,9},{9,10},{10,1... | collective-permute-start | bytes 786440 | tf_op jit(solution)/shard_map/ppermute | solution.py:25
  35.1 8.8 %collective-permute-start.1 = (bf16[1,256,512]{2,1,0:T(8,128)(2,1)S(1)}, bf16[1,256,512]{2,1,0:T(8,128)(2,1)S(1)}, u32[]{:S(2)}, u32[]{:S(2)}) collective-permute-start(bf16[1,256,512]{2,1,0:T(8,128)(2,1)S(1)} %get-tuple-element.2), channel_id=1, source_target_pairs={{1,0},{2,1},{3,2},{4,3},{5,4},{6,5},{7,6},{8,7},{9,8},{10,9},{11,1... | collective-permute-start | bytes 786440 | tf_op jit(solution)/shard_map/ppermute | solution.py:27
  40.5 4.5 copy-start.5
  44.9 1.5 copy-start.6
  52.8 9.5 %copy-start.7 = (bf16[256,256]{1,0:T(8,128)(2,1)S(1)}, bf16[256,256]{1,0:T(8,128)(2,1)}, u32[]{:S(2)}) copy-start(bf16[256,256]{1,0:T(8,128)(2,1)} %param.14) | copy-start | bytes 393220
  52.8 319.1 %all-to-all-start = ((bf16[16,4,4,64,512]{4,3,2,1,0:T(8,128)(2,1)}), bf16[16,4,4,64,512]{4,3,2,1,0:T(8,128)(2,1)}, u32[]{:S(2)}, u32[]{:S(2)}) async-start(bf16[16,4,4,64,512]{4,3,2,1,0:T(8,128)(2,1)} %stack.3), calls=%async_computation | async-start | bytes 33554432 | tf_op jit(solution)/shard_map/all_to_all | solution.py:124
  65.3 358.5 %copy-start.2 = (bf16[4,4,64,512]{2,0,3,1:T(4,128)(2,1)S(1)}, bf16[4,4,64,512]{2,0,3,1:T(4,128)(2,1)}, u32[]{:S(2)}) copy-start(bf16[4,4,64,512]{2,0,3,1:T(4,128)(2,1)} %copy.67) | copy-start | bytes 3145732
Sparse Core Ops, SparseCore 0:
  46.5 338.1 all-gather.1
